TPU v7x, 32 devices: a whole 2x2x4 slice. The times are simulated.
32 devices in a mesh: groups: 2 (over x), row: 16 (over z, y, core).
Axes of the slice: x: 2, y: 2, z: 4, core: 2. Of those that a mesh axis runs over, the one named last changes fastest.
Arguments:
- exterior_map: bfloat16 [15360, 7680], P(('groups', 'row')), parts along dimension 0, may hold values from -6 to 6
- couple_maps: bfloat16 [4, 7680, 1024], P('groups', 'row'), parts along dimension 0, may hold values from -0.1875 to 0.1875
- face_from_exterior: bfloat16 [15360, 1024], P(('groups', 'row')), parts along dimension 0, may hold values from -12 to 12
- face_maps: float32 [4096, 1024], P(('groups', 'row')), parts along dimension 0, may hold values from -1 to 2
- start_inverse: float32 [2048, 1024], P('groups'), parts along dimension 0, may hold values from -1 to 1
Outputs:
- merged_columns: bfloat16 [2, 15360, 7680], P(None, ('groups', 'row')), parts along dimension 1
There are 2 independent parts, one for each index of `groups`. A program takes and returns all parts, laid end to end along the dimension named above; each array names one. Nothing has to cross between parts.
All inputs are finite; a program needn't handle non-finite values.
Results may differ from a plain program's by a relative error of at most 0.0095.
Values may be sent and summed in bfloat16 or wider, within the bound.
A program may use at most 128 MiB of HBM per device.

v0:
```python
import jax
import jax.numpy as jnp
from jax import lax
from jax.sharding import PartitionSpec as P

NEWTON = 2


def shifted(block, axis, distance):
    devices = range(lax.axis_size(axis))
    route = [((i - distance) % len(devices), i) for i in devices]
    return lax.ppermute(block, axis, route)


def per_device(exterior_map, couple_maps, face_from_exterior, face_maps, start_inverse):
    high = lax.Precision.HIGHEST
    devices = lax.axis_size("row")
    position = lax.axis_index("row")
    halfway = devices // 2
    face_rows = face_maps.shape[0] // 2
    width = start_inverse.shape[0]
    sibling_side = position // halfway
    own_block = lax.dynamic_slice_in_dim(face_maps, sibling_side * face_rows, face_rows, 0)
    received = shifted(face_maps.astype(jnp.bfloat16), "row", halfway).astype(face_maps.dtype)
    coupling = own_block + lax.dynamic_slice_in_dim(
        received, sibling_side * face_rows, face_rows, 0
    )
    own_start = 2 * face_rows * (position % halfway) + face_rows * sibling_side

    def reorder(gathered):
        return (
            gathered.reshape(2, halfway, face_rows, width)
            .transpose(1, 0, 2, 3)
            .reshape(width, width)
        )

    iterate = start_inverse
    product = iterate
    for newton_step in range(NEWTON):
        product_rows = jnp.dot(
            coupling, iterate, precision=high, preferred_element_type=jnp.float32
        )
        product = reorder(lax.all_gather(product_rows, "row", axis=0, tiled=True))
        if newton_step + 1 < NEWTON:
            my_rows = lax.dynamic_slice_in_dim(iterate, own_start, face_rows, 0)
            next_rows = 2.0 * my_rows - jnp.dot(
                my_rows, product, precision=high, preferred_element_type=jnp.float32
            )
            iterate = reorder(
                lax.all_gather(next_rows.astype(jnp.bfloat16), "row", axis=0, tiled=True).astype(
                    next_rows.dtype
                )
            )
    panel_rows = face_from_exterior.astype(jnp.float32)
    contract = (((1,), (1,)), ((), ()))
    direct = lax.dot_general(
        panel_rows, iterate, contract, precision=high, preferred_element_type=jnp.float32
    )
    through = lax.dot_general(
        panel_rows, product, contract, precision=high, preferred_element_type=jnp.float32
    )
    image_rows = 2.0 * direct - lax.dot_general(
        through, iterate, contract, precision=high, preferred_element_type=jnp.float32
    )
    image_rows = image_rows.astype(jnp.bfloat16)
    own_cols = exterior_map.astype(jnp.float32)
    update = jnp.einsum(
        "bis,es->bie",
        couple_maps,
        lax.all_gather(image_rows, "row", axis=0, tiled=True),
        preferred_element_type=jnp.float32,
    )
    return jnp.stack([own_cols - update[0], -update[1]]).astype(jnp.bfloat16)


def solution(mesh):
    return jax.shard_map(
        per_device,
        mesh=mesh,
        in_specs=(
            P(("groups", "row"), None),
            P("groups", "row", None),
            P(("groups", "row"), None),
            P(("groups", "row"), None),
            P("groups", None),
        ),
        out_specs=P(None, ("groups", "row"), None),
        check_vma=False,
    )
```

profile of v0, /device:TPU:0, one launch (start us, length us, event | category | flops | bytes accessed | tf_op | source)
XLA Modules:
  0.0 371.5 jit_solution(8878733400885816180)
XLA Ops:
  6.5 1.2 convert_element_type.19
  7.8 4.1 %collective-permute-start = (bf16[128,1024]{1,0:T(8,128)(2,1)S(1)}, bf16[128,1024]{1,0:T(8,128)(2,1)S(1)}, u32[]{:S(2)}, u32[]{:S(2)}) collective-permute-start(bf16[128,1024]{1,0:T(8,128)(2,1)S(1)} %convert_element_type.19), channel_id=1, source_target_pairs={{8,0},{9,1},{10,2},{11,3},{12,4},{13,5},{14,6},{15,7},{0,8},{1,9},... | collective-permute-start | bytes 786440 | tf_op jit(solution)/shard_map/ppermute | solution.py:12
  11.9 11.9 %collective-permute-done = bf16[128,1024]{1,0:T(8,128)(2,1)S(1)} collective-permute-done((bf16[128,1024]{1,0:T(8,128)(2,1)S(1)}, bf16[128,1024]{1,0:T(8,128)(2,1)S(1)}, u32[]{:S(2)}, u32[]{:S(2)}) %collective-permute-start) | collective-permute-done | bytes 262176 | tf_op jit(solution)/shard_map/ppermute | solution.py:12
  23.8 5.6 %fusion.9 = f32[64,1024]{1,0:T(8,128)} fusion(f32[1024,1024]{1,0:T(8,128)} %param.9, f32[128,1024]{1,0:T(8,128)} %param.8, s32[]{:T(128)S(6)} %select_n.21, bf16[128,1024]{1,0:T(8,128)(2,1)S(1)} %collective-permute-done), kind=kOutput, calls=%fused_computation.16 | convolution fusion | flops 805437440 | bytes 4849668 | tf_op jit(solution)/shard_map/dot_general | solution.py:40
  29.4 0.0 all-gather.7.cloned.1.call-start
  29.5 51.8 %all-gather.5.cloned.1.call-done = f32[1024,1024]{1,0:T(8,128)} async-done(((f32[64,1024]{1,0:T(8,128)}), f32[1024,1024]{1,0:T(8,128)}) %all-gather.5.cloned.1.call-update) | async-done | bytes 4194320 | tf_op jit(solution)/shard_map/all_gather | solution.py:43
  81.3 2.5 copy.6
  83.8 4.4 %fusion.6 = bf16[64,1024]{1,0:T(8,128)(2,1)} fusion(f32[1024,1024]{1,0:T(8,128)S(1)} %bitcast.42, f32[1024,1024]{1,0:T(8,128)} %param.9, s32[]{:T(128)S(6)} %select_n.20), kind=kOutput, calls=%fused_computation.12 | convolution fusion | flops 805502976 | bytes 4850688 | tf_op jit(solution)/shard_map/dot_general | solution.py:46
  88.3 40.0 %all-gather.7.cloned.1.call-done = bf16[1024,1024]{1,0:T(8,128)(2,1)} async-done(((bf16[64,1024]{1,0:T(8,128)(2,1)}), bf16[1024,1024]{1,0:T(8,128)(2,1)}) %all-gather.7.cloned.1.call-update) | async-done | bytes 2097168 | tf_op jit(solution)/shard_map/all_gather | solution.py:50
  128.3 1.8 copy.7
  130.1 1.3 copy-done.3
  131.4 1.9 fusion.8
  133.4 0.2 all-gather.11.cloned.1.call-start
  133.6 49.3 %all-gather.9.cloned.1.call-done = f32[1024,1024]{1,0:T(8,128)} async-done(((f32[64,1024]{1,0:T(8,128)}), f32[1024,1024]{1,0:T(8,128)}) %all-gather.9.cloned.1.call-update) | async-done | bytes 4194320 | tf_op jit(solution)/shard_map/all_gather | solution.py:43
  182.9 2.6 copy.8
  185.5 3.4 fusion.15
  188.9 6.7 %fusion.16 = f32[480,1024]{1,0:T(8,128)S(1)} fusion(f32[1024,480]{1,0:T(8,128)S(1)} %fusion.15, bf16[1024,1024]{1,0:T(8,128)(2,1)S(1)} %bitcast.44), kind=kOutput, calls=%fused_computation.23 | convolution fusion | flops 6039797760 | bytes 6029312 | tf_op jit(solution)/shard_map/dot_general | solution.py:62
  195.7 2.2 fusion.5
  197.9 119.0 %all-gather.11.cloned.1.call-done = bf16[7680,1024]{1,0:T(8,128)(2,1)} async-done(((bf16[480,1024]{1,0:T(8,128)(2,1)}), bf16[7680,1024]{1,0:T(8,128)(2,1)}) %all-gather.11.cloned.1.call-update) | async-done | bytes 15728656 | tf_op jit(solution)/shard_map/all_gather | solution.py:70
  316.8 22.8 %convolution_bitcast_fusion = f32[2,480,7680]{2,1,0:T(8,128)} fusion(bf16[2,480,1024]{2,1,0:T(8,128)(2,1)S(1)} %copy-done, bf16[7680,1024]{1,0:T(8,128)(2,1)} %all-gather.11.cloned.1.call-done), kind=kOutput, calls=%fused_computation | convolution fusion | flops 15099494400 | bytes 47185920 | tf_op jit(solution)/shard_map/bis,es->bie/dot_general | solution.py:67
  339.6 9.6 %fusion.1 = bf16[1,480,7680]{2,1,0:T(8,128)(2,1)} fusion(f32[2,480,7680]{2,1,0:T(8,128)} %convolution_bitcast_fusion), kind=kLoop, calls=%fused_computation.3 | loop fusion | flops 7372800 | bytes 22118400 | tf_op jit(solution)/shard_map/convert.1
  349.3 8.1 %fusion.4 = bf16[1,480,7680]{2,1,0:T(8,128)(2,1)S(1)} fusion(f32[2,480,7680]{2,1,0:T(8,128)} %convolution_bitcast_fusion, bf16[480,7680]{1,0:T(8,128)(2,1)} %param.5), kind=kLoop, calls=%fused_computation.8 | loop fusion | flops 11059200 | bytes 29491200 | tf_op jit(solution)/shard_map/stack | solution.py:73
  357.3 1.4 copy-done.2
  358.7 6.2 %pad_maximum_fusion = bf16[2,480,7680]{2,1,0:T(8,128)(2,1)} fusion(bf16[1,480,7680]{2,1,0:T(8,128)(2,1)S(1)} %copy-done.2, bf16[1,480,7680]{2,1,0:T(8,128)(2,1)S(1)} %fusion.4), kind=kLoop, calls=%fused_computation.7 | loop fusion | flops 7372800 | bytes 29491200 | tf_op jit(solution)/shard_map/stack | solution.py:73
  (18 shorter events, 0.1 us)
Async XLA Ops:
  6.5 310.3 %copy-start = (bf16[2,480,1024]{2,1,0:T(8,128)(2,1)S(1)}, bf16[2,480,1024]{2,1,0:T(8,128)(2,1)}, u32[]{:S(2)}) copy-start(bf16[2,480,1024]{2,1,0:T(8,128)(2,1)} %param.6) | copy-start | bytes 5898244
  6.5 74.8 %all-gather.5.cloned.1.call-start = ((), (), s32[]{:S(2)}) async-start(), calls=%async_computation | async-start | bytes 4456448 | tf_op jit(solution)/shard_map/all_gather | solution.py:43
  7.8 16.0 %collective-permute-start = (bf16[128,1024]{1,0:T(8,128)(2,1)S(1)}, bf16[128,1024]{1,0:T(8,128)(2,1)S(1)}, u32[]{:S(2)}, u32[]{:S(2)}) collective-permute-start(bf16[128,1024]{1,0:T(8,128)(2,1)S(1)} %convert_element_type.19), channel_id=1, source_target_pairs={{8,0},{9,1},{10,2},{11,3},{12,4},{13,5},{14,6},{15,7},{0,8},{1,9},... | collective-permute-start | bytes 786440 | tf_op jit(solution)/shard_map/ppermute | solution.py:12
  29.4 98.9 %all-gather.7.cloned.1.call-start = ((), (), s32[]{:S(2)}) async-start(), calls=%async_computation.1 | async-start | bytes 2228224 | tf_op jit(solution)/shard_map/all_gather | solution.py:50
  83.8 47.6 %copy-start.5 = (f32[128,1024]{1,0:T(8,128)S(1)}, f32[128,1024]{1,0:T(8,128)}, u32[]{:S(2)}) copy-start(f32[128,1024]{1,0:T(8,128)} %param.8) | copy-start | bytes 1572868
  88.3 94.6 %all-gather.9.cloned.1.call-start = ((), (), s32[]{:S(2)}) async-start(), calls=%async_computation.2 | async-start | bytes 4456448 | tf_op jit(solution)/shard_map/all_gather | solution.py:43
  130.1 1.3 copy-start.3
  133.4 183.4 %all-gather.11.cloned.1.call-start = ((), (), s32[]{:S(2)}) async-start(), calls=%async_computation.3 | async-start | bytes 16711680 | tf_op jit(solution)/shard_map/all_gather | solution.py:70
  182.9 2.6 copy-start.6
  185.5 3.5 copy-start.4
  349.3 9.5 %copy-start.2 = (bf16[1,480,7680]{2,1,0:T(8,128)(2,1)S(1)}, bf16[1,480,7680]{2,1,0:T(8,128)(2,1)}, u32[]{:S(2)}) copy-start(bf16[1,480,7680]{2,1,0:T(8,128)(2,1)} %fusion.1) | copy-start | bytes 22118404
  358.7 6.2 %copy-start.1 = (bf16[2,480,1024]{2,1,0:T(8,128)(2,1)S(1)}, bf16[2,480,1024]{2,1,0:T(8,128)(2,1)}, u32[]{:S(2)}) copy-start(bf16[2,480,1024]{2,1,0:T(8,128)(2,1)} %param.6) | copy-start | bytes 5898244
Sparse Core Ops, SparseCore 0:
  29.6 51.7 all-gather.4
  88.4 39.8 all-gather.6
  133.5 49.3 all-gather.8
  198.0 118.7 all-gather.10
where the time goes:
time: 372 us; the launch traced here: 371 us
  waiting for transfers between devices  272 us (73%)
  matrix products  47.1 us (13%)
  other arithmetic  25.1 us (7%)
  between operations  13.2 us (4%)
  local copies, waits for them, and re-layouts  9.56 us (3%)
  starting transfers between devices  4.41 us (1%)
    all_gather x1, waiting for transfers between devices, per_device(): lax.all_gather(image_rows, 'row', axis=0, tiled=True)  119 us
    all_gather x2, waiting for transfers between devices, per_device(): product = reorder(lax.all_gather(product_rows, 'row', axis=0, tiled=True))  101 us
    all_gather x1, waiting for transfers between devices, per_device(): lax.all_gather(next_rows.astype(jnp.bfloat16), 'row', axis=0, tiled=True)  40 us
    dot_general x1, matrix products, per_device(): jnp.einsum('bis,es->bie', couple_maps, lax.all_gather(image_rows, 'row',...  22.8 us
    another operation x2, other arithmetic, per_device(): return jnp.stack([own_cols - update[0], -update[1]]).astype(jnp.bfloat16)  14.3 us
    ppermute x1, waiting for transfers between devices, shifted(): return lax.ppermute(block, axis, route)  11.9 us
    another operation x1, other arithmetic  9.64 us
    dot_general x2, matrix products, per_device(): jnp.dot(coupling, iterate, precision=high, preferred_element_type=jnp.flo...  7.58 us
  transfers between devices with their start and end apart: 5, of which 5 were waited for; matrix products, arithmetic and copies ran while one was open for 0% of the time, Pallas kernels for 0%

commit v1 on v0

v1 whole, which is shorter than its diff:
```python
import jax
import jax.numpy as jnp
from jax import lax
from jax.sharding import PartitionSpec as P


def per_device(exterior_map, couple_maps, face_from_exterior, face_maps, start_inverse):
    high = lax.Precision.HIGHEST
    f32 = jnp.float32
    bf16 = jnp.bfloat16
    devices = lax.axis_size("row")
    position = lax.axis_index("row")
    halfway = devices // 2
    width = start_inverse.shape[0]
    rows = face_maps.shape[0] // 2
    side = position // halfway
    panels = lax.all_gather(face_from_exterior, "row", axis=0, tiled=True)
    mine = lax.dynamic_slice_in_dim(face_maps, side * rows, rows, 0)
    theirs = lax.dynamic_slice_in_dim(face_maps, (1 - side) * rows, rows, 0)
    route = [((i - halfway) % devices, i) for i in range(devices)]
    received = lax.ppermute(theirs.astype(bf16), "row", route).astype(f32)
    coupling = mine + received
    start = 2 * rows * (position % halfway) + rows * side
    product = jnp.dot(coupling, start_inverse, precision=high, preferred_element_type=f32)
    row_index = start + lax.broadcasted_iota(jnp.int32, product.shape, 0)
    col_index = lax.broadcasted_iota(jnp.int32, product.shape, 1)
    residual = (row_index == col_index).astype(f32) - product
    gathered = lax.all_gather(residual.astype(bf16), "row", axis=0, tiled=True)
    residual = gathered.reshape(2, halfway, rows, width).transpose(1, 0, 2, 3).reshape(width, width)
    maps = couple_maps.reshape(-1, width)
    first = jnp.dot(maps.astype(f32), start_inverse, precision=lax.Precision.HIGH, preferred_element_type=f32)
    square = jnp.dot(residual, residual, preferred_element_type=f32).astype(bf16)
    second = first + jnp.dot(first.astype(bf16), residual, preferred_element_type=f32)
    third = second + jnp.dot(second.astype(bf16), square, preferred_element_type=f32)
    left = third.astype(bf16).reshape(couple_maps.shape)
    update = jnp.einsum("bis,es->bie", left, panels, preferred_element_type=f32)
    return jnp.stack([exterior_map.astype(f32) - update[0], -update[1]]).astype(bf16)


def solution(mesh):
    return jax.shard_map(
        per_device,
        mesh=mesh,
        in_specs=(
            P(("groups", "row"), None),
            P("groups", "row", None),
            P(("groups", "row"), None),
            P(("groups", "row"), None),
            P("groups", None),
        ),
        out_specs=P(None, ("groups", "row"), None),
        check_vma=False,
    )
```

time: 372 us -> 243 us (0.65)
  waiting for transfers between devices: 272 us -> 143 us
  matrix products: 47.1 us -> 52.8 us
  local copies, waits for them, and re-layouts: 9.56 us -> 5.75 us
    all_gather x4 -> x2, waiting for transfers between devices: 260 us -> 136 us  [the longest x1 102 us: per_device(): panels = lax.all_gather(face_from_exterior, 'row', axis=0, tiled=True)]
    dot_general x7 -> x5, matrix products: 47.1 us -> 52.8 us  [the longest x1 22.8 us: per_device(): update = jnp.einsum('bis,es->bie', left, panels, preferred_element_type=f32)]
    ppermute x1, waiting for transfers between devices: 11.9 us -> 6.3 us  [per_device(): received = lax.ppermute(theirs.astype(bf16), 'row', route).astype(f32)]
    reshape x3 -> x1, local copies, waits for them, and re-layouts: 6.84 us -> 1.91 us  [per_device(): gathered.reshape(2, halfway, rows, width).transpose(1, 0, 2, 3)]
  transfers between devices with their start and end apart: 5 -> 3, of which waited for: 5 -> 3; matrix products, arithmetic and copies ran while one was open for 0% -> 11% of each run, Pallas kernels for 0% -> 0%
where the time goes in v1:
time: 243 us
  waiting for transfers between devices  143 us (59%)
  matrix products  52.8 us (22%)
  other arithmetic  23.9 us (10%)
  between operations  13.5 us (6%)
  local copies, waits for them, and re-layouts  5.75 us (2%)
  starting transfers between devices  4.15 us (2%)
    all_gather x1, waiting for transfers between devices, per_device(): panels = lax.all_gather(face_from_exterior, 'row', axis=0, tiled=True)  102 us
    all_gather x1, waiting for transfers between devices, per_device(): gathered = lax.all_gather(residual.astype(bf16), 'row', axis=0, tiled=True)  33.6 us
    dot_general x1, matrix products, per_device(): update = jnp.einsum('bis,es->bie', left, panels, preferred_element_type=f32)  22.8 us
    another operation x2, other arithmetic, per_device(): jnp.stack([exterior_map.astype(f32) - update[0], -update[1]]).astype(bf16)  14.3 us
    dot_general x1, matrix products, per_device(): jnp.dot(second.astype(bf16), square, preferred_element_type=f32)  12.1 us
    another operation x1, other arithmetic  9.64 us
    dot_general x1, matrix products, per_device(): jnp.dot(maps.astype(f32), start_inverse, precision=lax.Precision.HIGH, pr...  8.35 us
    ppermute x1, waiting for transfers between devices, per_device(): received = lax.ppermute(theirs.astype(bf16), 'row', route).astype(f32)  6.3 us
  transfers between devices with their start and end apart: 3, of which 3 were waited for; matrix products, arithmetic and copies ran while one was open for 11% of the time, Pallas kernels for 0%

profile of v1, /device:TPU:0, one launch (start us, length us, event | category | flops | bytes accessed | tf_op | source)
XLA Modules:
  0.0 242.7 jit_solution(1649933608703926377)
XLA Ops:
  6.5 0.0 copy-start
  6.5 0.0 all-gather.3.cloned.1.call-start
  6.5 1.1 dynamic-slice_convert_fusion
  7.6 4.1 %collective-permute-start = (bf16[64,1024]{1,0:T(8,128)(2,1)S(1)}, bf16[64,1024]{1,0:T(8,128)(2,1)S(1)}, u32[]{:S(2)}, u32[]{:S(2)}) collective-permute-start(bf16[64,1024]{1,0:T(8,128)(2,1)S(1)} %dynamic-slice_convert_fusion), channel_id=1, source_target_pairs={{8,0},{9,1},{10,2},{11,3},{12,4},{13,5},{14,6},{15,7},{0,8},{1,9},... | collective-permute-start | bytes 393224 | tf_op jit(solution)/shard_map/ppermute | solution.py:21
  11.8 6.3 %collective-permute-done = bf16[64,1024]{1,0:T(8,128)(2,1)S(1)} collective-permute-done((bf16[64,1024]{1,0:T(8,128)(2,1)S(1)}, bf16[64,1024]{1,0:T(8,128)(2,1)S(1)}, u32[]{:S(2)}, u32[]{:S(2)}) %collective-permute-start) | collective-permute-done | bytes 131104 | tf_op jit(solution)/shard_map/ppermute | solution.py:21
  18.1 5.6 %fusion.16 = bf16[64,1024]{1,0:T(8,128)(2,1)} fusion(f32[1024,1024]{1,0:T(8,128)} %param.9, bf16[64,1024]{1,0:T(8,128)(2,1)S(1)} %collective-permute-done, f32[128,1024]{1,0:T(8,128)} %param.8, s32[]{:T(128)S(6)} %select_n.19, s32[64]{0:T(128)S(1)} %iota_add_fusion), kind=kOutput, calls=%fused_computation.17 | convolution fusion | flops 805699584 | bytes 4718852 | tf_op jit(solution)/shard_map/dot_general | solution.py:24
  23.6 0.0 all-gather.3.cloned.1.call-update
  23.7 0.0 all-gather.5.cloned.1.call-start
  23.7 0.7 all-gather.5.cloned.1.call-update
  24.4 0.0 copy-done
  24.4 8.3 %fusion.23 = f32[960,1024]{1,0:T(8,128)} fusion(bf16[960,1024]{1,0:T(8,128)(2,1)S(1)} %bitcast.26, f32[1024,1024]{1,0:T(8,128)} %param.9), kind=kOutput, calls=%fused_computation.26 | convolution fusion | flops 6039797760 | bytes 10092544 | tf_op jit(solution)/shard_map/dot_general | solution.py:31
  32.8 33.6 %all-gather.3.cloned.1.call-done = bf16[1024,1024]{1,0:T(8,128)(2,1)} async-done(((bf16[64,1024]{1,0:T(8,128)(2,1)}), bf16[1024,1024]{1,0:T(8,128)(2,1)}) %all-gather.3.cloned.1.call-update) | async-done | bytes 2097168 | tf_op jit(solution)/shard_map/all_gather | solution.py:28
  66.4 1.9 copy.6
  68.3 0.0 copy-start.3
  68.3 1.3 copy-done.3
  69.7 0.0 copy-done.4
  69.7 4.1 %fusion.14 = f32[960,1024]{1,0:T(8,128)} fusion(bf16[1024,1024]{1,0:T(8,128)(2,1)S(1)} %bitcast.28, f32[960,1024]{1,0:T(8,128)S(1)} %copy-done.4), kind=kOutput, calls=%fused_computation.14 | convolution fusion | flops 2014248960 | bytes 9961472 | tf_op jit(solution)/shard_map/dot_general | solution.py:33
  73.7 12.1 %add_convert_fusion = bf16[960,1024]{1,0:T(8,128)(2,1)S(1)} fusion(f32[960,1024]{1,0:T(8,128)} %fusion.23, f32[960,1024]{1,0:T(8,128)} %fusion.14, bf16[1024,1024]{1,0:T(8,128)(2,1)} %bitcast.29), kind=kOutput, calls=%fused_computation.9 | convolution fusion | flops 4166713344 | bytes 11927552 | tf_op jit(solution)/shard_map/dot_general | solution.py:34
  85.8 102.0 %all-gather.5.cloned.1.call-done = bf16[7680,1024]{1,0:T(8,128)(2,1)} async-done(((bf16[480,1024]{1,0:T(8,128)(2,1)}), bf16[7680,1024]{1,0:T(8,128)(2,1)}) %all-gather.5.cloned.1.call-update) | async-done | bytes 15728656 | tf_op jit(solution)/shard_map/all_gather | solution.py:17
  187.8 22.8 %fusion = f32[2,480,7680]{2,1,0:T(8,128)} fusion(bf16[2,480,1024]{2,1,0:T(8,128)(2,1)S(1)} %bitcast.30, bf16[7680,1024]{1,0:T(8,128)(2,1)} %all-gather.5.cloned.1.call-done), kind=kOutput, calls=%fused_computation | convolution fusion | flops 15099494400 | bytes 47185920 | tf_op jit(solution)/shard_map/bis,es->bie/dot_general | solution.py:36
  210.6 9.6 %fusion.2 = bf16[1,480,7680]{2,1,0:T(8,128)(2,1)} fusion(f32[2,480,7680]{2,1,0:T(8,128)} %fusion), kind=kLoop, calls=%fused_computation.3 | loop fusion | flops 7372800 | bytes 22118400 | tf_op jit(solution)/shard_map/convert.1
  220.2 8.1 %fusion.5 = bf16[1,480,7680]{2,1,0:T(8,128)(2,1)S(1)} fusion(f32[2,480,7680]{2,1,0:T(8,128)} %fusion, bf16[480,7680]{1,0:T(8,128)(2,1)} %param.5), kind=kLoop, calls=%fused_computation.8 | loop fusion | flops 11059200 | bytes 29491200 | tf_op jit(solution)/shard_map/stack | solution.py:37
  228.3 1.4 copy-done.2
  229.7 6.2 %pad_maximum_fusion = bf16[2,480,7680]{2,1,0:T(8,128)(2,1)} fusion(bf16[1,480,7680]{2,1,0:T(8,128)(2,1)S(1)} %copy-done.2, bf16[1,480,7680]{2,1,0:T(8,128)(2,1)S(1)} %fusion.5), kind=kLoop, calls=%fused_computation.7 | loop fusion | flops 7372800 | bytes 29491200 | tf_op jit(solution)/shard_map/stack | solution.py:37
  (5 shorter events, 0.0 us)
Async XLA Ops:
  6.5 17.9 %copy-start = (bf16[2,480,1024]{2,1,0:T(8,128)(2,1)S(1)}, bf16[2,480,1024]{2,1,0:T(8,128)(2,1)}, u32[]{:S(2)}) copy-start(bf16[2,480,1024]{2,1,0:T(8,128)(2,1)} %param.6) | copy-start | bytes 5898244
  6.5 59.9 %all-gather.3.cloned.1.call-start = ((), (), s32[]{:S(2)}) async-start(), calls=%async_computation | async-start | bytes 2228224 | tf_op jit(solution)/shard_map/all_gather | solution.py:28
  7.6 10.4 %collective-permute-start = (bf16[64,1024]{1,0:T(8,128)(2,1)S(1)}, bf16[64,1024]{1,0:T(8,128)(2,1)S(1)}, u32[]{:S(2)}, u32[]{:S(2)}) collective-permute-start(bf16[64,1024]{1,0:T(8,128)(2,1)S(1)} %dynamic-slice_convert_fusion), channel_id=1, source_target_pairs={{8,0},{9,1},{10,2},{11,3},{12,4},{13,5},{14,6},{15,7},{0,8},{1,9},... | collective-permute-start | bytes 393224 | tf_op jit(solution)/shard_map/ppermute | solution.py:21
  23.7 164.1 %all-gather.5.cloned.1.call-start = ((), (), s32[]{:S(2)}) async-start(), calls=%async_computation.1 | async-start | bytes 16711680 | tf_op jit(solution)/shard_map/all_gather | solution.py:17
  66.4 3.3 %copy-start.4 = (f32[960,1024]{1,0:T(8,128)S(1)}, f32[960,1024]{1,0:T(8,128)}, u32[]{:S(2)}) copy-start(f32[960,1024]{1,0:T(8,128)} %fusion.23) | copy-start | bytes 11796484
  68.3 1.3 copy-start.3
  220.2 9.5 %copy-start.2 = (bf16[1,480,7680]{2,1,0:T(8,128)(2,1)S(1)}, bf16[1,480,7680]{2,1,0:T(8,128)(2,1)}, u32[]{:S(2)}) copy-start(bf16[1,480,7680]{2,1,0:T(8,128)(2,1)} %fusion.2) | copy-start | bytes 22118404
  229.7 6.2 %copy-start.1 = (bf16[2,480,1024]{2,1,0:T(8,128)(2,1)S(1)}, bf16[2,480,1024]{2,1,0:T(8,128)(2,1)}, u32[]{:S(2)}) copy-start(bf16[2,480,1024]{2,1,0:T(8,128)(2,1)} %param.6) | copy-start | bytes 5898244
Sparse Core Ops, SparseCore 0:
  23.8 42.5 all-gather.2
  68.7 119.0 all-gather.4

commit v2 on v1

v2 whole, which is shorter than its diff:
```python
import functools

import jax
import jax.numpy as jnp
from jax import lax
from jax.experimental import pallas as pl
from jax.experimental.pallas import tpu as pltpu
from jax.sharding import PartitionSpec as P

F32 = jnp.float32
BF16 = jnp.bfloat16
LANES = 128
RIGHT, LEFT, ACROSS, CORE_OWN, CORE_OTHER = range(5)


def tile_width(span):
    return max(w for w in range(LANES, 641, LANES) if span % w == 0)


def kernel(
    n,
    ext_ref,
    maps_ref,
    panel_ref,
    face_ref,
    start_ref,
    out_ref,
    panels,
    resid,
    ext,
    maps,
    start,
    start_hi,
    start_lo,
    image,
    left,
    square,
    stage,
    face_out,
    face_in,
    local_sem,
    out_sem,
    face_sem,
    send_sem,
    recv_sem,
):
    line = n // 4
    halfway = n // 2
    block = panel_ref.shape[0]
    half = face_ref.shape[0] // 2
    width = start.shape[0]
    me = lax.axis_index("row")
    z, y, c = me // 4, (me // 2) % 2, me % 2
    side = me // halfway
    sibling = (me + halfway) % n
    has_right, has_left = z < line - 1, z > 0

    def device(zz, yy, cc):
        return zz * 4 + yy * 2 + cc

    local = [
        pltpu.make_async_copy(start_ref, start, local_sem.at[0]),
        pltpu.make_async_copy(maps_ref, maps, local_sem.at[1]),
        pltpu.make_async_copy(
            panel_ref,
            panels.at[pl.ds(pl.multiple_of(me * block, 16), block)],
            local_sem.at[2],
        ),
        pltpu.make_async_copy(ext_ref, ext, local_sem.at[3]),
    ]
    for copy in local:
        copy.start()

    barrier = pltpu.get_barrier_semaphore()

    def greet(target):
        pl.semaphore_signal(
            barrier, inc=1, device_id={"row": target}, device_id_type=pl.DeviceIdType.MESH
        )

    greet(device(z, 1 - y, c))
    greet(device(z, y, 1 - c))
    greet(sibling)

    @pl.when(has_right)
    def _():
        greet(me + 4)

    @pl.when(has_left)
    def _():
        greet(me - 4)

    face_out[...] = face_ref[pl.ds(pl.multiple_of((1 - side) * half, 16), half)].astype(BF16)
    pl.semaphore_wait(barrier, 3 + has_right.astype(jnp.int32) + has_left.astype(jnp.int32))

    exchange = pltpu.make_async_remote_copy(
        src_ref=face_out,
        dst_ref=face_in,
        send_sem=face_sem.at[0],
        recv_sem=face_sem.at[1],
        device_id={"row": sibling},
        device_id_type=pl.DeviceIdType.MESH,
    )
    exchange.start()

    def panel_rows(dev):
        return panels.at[pl.ds(pl.multiple_of(dev * block, 16), block)]

    def resid_start(dev):
        return pl.multiple_of((2 * (dev % halfway) + dev // halfway) * half, 16)

    def resid_rows(dev):
        return resid.at[pl.ds(resid_start(dev), half)]

    def copy_of(kind, rows_of, way, dev, source=None):
        target = {
            RIGHT: me + 4,
            LEFT: me - 4,
            ACROSS: device(z, 1 - y, c),
            CORE_OWN: device(z, y, 1 - c),
            CORE_OTHER: device(z, y, 1 - c),
        }[way]
        return pltpu.make_async_remote_copy(
            src_ref=rows_of(dev) if source is None else source,
            dst_ref=rows_of(dev),
            send_sem=send_sem.at[kind, way, dev // 4],
            recv_sem=recv_sem.at[kind, dev],
            device_id={"row": target},
            device_id_type=pl.DeviceIdType.MESH,
        )

    def relay(kind, rows_of):
        def send_own(source):
            copy_of(kind, rows_of, ACROSS, me, source).start()

            @pl.when(has_right)
            def _():
                copy_of(kind, rows_of, RIGHT, me, source).start()

            @pl.when(has_left)
            def _():
                copy_of(kind, rows_of, LEFT, me, source).start()

            copy_of(kind, rows_of, CORE_OWN, me, source).start()

        def wait(dev):
            copy_of(kind, rows_of, CORE_OWN, dev).wait_recv()

        def at_step(step, act):
            if step == 0:
                act(z)
            else:

                @pl.when(z >= step)
                def _():
                    act(z - step)

                @pl.when(z + step < line)
                def _():
                    act(z + step)

        def along(step):
            @pl.when(z >= step)
            def _():
                dev = device(z - step, y, c)
                wait(dev)

                @pl.when(has_right)
                def _():
                    copy_of(kind, rows_of, RIGHT, dev).start()

                copy_of(kind, rows_of, ACROSS, dev).start()
                copy_of(kind, rows_of, CORE_OWN, dev).start()

            @pl.when(z + step < line)
            def _():
                dev = device(z + step, y, c)
                wait(dev)

                @pl.when(has_left)
                def _():
                    copy_of(kind, rows_of, LEFT, dev).start()

                copy_of(kind, rows_of, ACROSS, dev).start()
                copy_of(kind, rows_of, CORE_OWN, dev).start()

        def across(step):
            def act(zz):
                dev = device(zz, 1 - y, c)
                wait(dev)
                copy_of(kind, rows_of, CORE_OTHER, dev).start()

            at_step(step, act)

        def core(step):
            def act(zz):
                wait(device(zz, y, 1 - c))
                wait(device(zz, 1 - y, 1 - c))

            at_step(step, act)

        def finish():
            @pl.loop(0, line)
            def _(zz):
                dev = device(zz, y, c)

                @pl.when(has_right & (zz <= z))
                def _():
                    copy_of(kind, rows_of, RIGHT, dev).wait_send()

                @pl.when(has_left & (zz >= z))
                def _():
                    copy_of(kind, rows_of, LEFT, dev).wait_send()

                copy_of(kind, rows_of, ACROSS, dev).wait_send()
                copy_of(kind, rows_of, CORE_OWN, dev).wait_send()
                copy_of(kind, rows_of, CORE_OTHER, device(zz, 1 - y, c)).wait_send()

        return send_own, along, across, core, finish, at_step

    send_panel, panel_along, panel_across, panel_core, panel_finish, at_step = relay(0, panel_rows)
    send_resid, resid_along, resid_across, resid_core, resid_finish, _ = relay(1, resid_rows)

    send_panel(panel_ref)

    local[0].wait()
    start_hi[...] = start[...].astype(BF16)
    start_lo[...] = (start[...] - start_hi[...].astype(F32)).astype(BF16)
    exchange.wait()
    coupling = face_ref[pl.ds(pl.multiple_of(side * half, 16), half)] + face_in[...].astype(F32)
    coupling_hi = coupling.astype(BF16)
    coupling_lo = (coupling - coupling_hi.astype(F32)).astype(BF16)
    product = jnp.dot(coupling_hi, start_hi[...], preferred_element_type=F32)
    product += jnp.dot(coupling_hi, start_lo[...], preferred_element_type=F32)
    product += jnp.dot(coupling_lo, start_hi[...], preferred_element_type=F32)
    first = resid_start(me)
    row_index = first + lax.broadcasted_iota(jnp.int32, product.shape, 0)
    col_index = lax.broadcasted_iota(jnp.int32, product.shape, 1)
    identity = jnp.where(row_index == col_index, 1.0, 0.0)
    resid[pl.ds(first, half)] = (identity - product).astype(BF16)
    send_resid(resid_rows(me))

    local[1].wait()

    @pl.loop(0, 2)
    def _(box):
        image[box] = jnp.dot(
            maps[box], start_hi[...], preferred_element_type=F32
        ) + jnp.dot(maps[box], start_lo[...], preferred_element_type=F32)

    for step in range(1, line):
        resid_along(step)
    panel_along(1)
    for step in range(line):
        resid_across(step)
    for step in range(line):
        resid_core(step)

    square_rows = width // 4

    @pl.loop(0, 4)
    def _(part):
        rows = pl.ds(pl.multiple_of(part * square_rows, 16), square_rows)
        square[rows] = jnp.dot(resid[rows], resid[...], preferred_element_type=F32).astype(BF16)

    @pl.loop(0, 2)
    def _(box):
        value = image[box]
        value += jnp.dot(value.astype(BF16), resid[...], preferred_element_type=F32)
        value += jnp.dot(value.astype(BF16), square[...], preferred_element_type=F32)
        left[box] = value.astype(BF16)

    local[2].wait()
    local[3].wait()

    def columns(begin, span):
        tile = stage.shape[-1]
        tiles = span // tile

        def copy_out(at, slot):
            at = pl.multiple_of(at, LANES)
            return pltpu.make_async_copy(
                stage.at[slot], out_ref.at[:, :, pl.ds(at, tile)], out_sem.at[slot]
            )

        @pl.loop(0, tiles)
        def _(index):
            slot = index % 2
            at = pl.multiple_of(begin + index * tile, LANES)

            @pl.when(index >= 2)
            def _():
                copy_out(at, slot).wait()

            part = panels[pl.ds(at, tile)]
            contract = (((1,), (1,)), ((), ()))
            upper = lax.dot_general(left[0], part, contract, preferred_element_type=F32)
            stage[slot, 0] = (ext[:, pl.ds(at, tile)].astype(F32) - upper).astype(BF16)
            lower = lax.dot_general(left[1], part, contract, preferred_element_type=F32)
            stage[slot, 1] = (-lower).astype(BF16)
            copy_out(at, slot).start()

        for index in range(max(tiles - 2, 0), tiles):
            copy_out(begin, index % 2).wait()

    group = 4 * block
    aligned = group % LANES == 0
    for step in range(line):
        if step > 0 and step + 1 < line:
            panel_along(step + 1)
        panel_across(step)
        panel_core(step)
        if aligned:
            at_step(step, lambda zz: columns(zz * group, group))
    if not aligned:
        columns(0, panels.shape[0])

    panel_finish()
    resid_finish()


def per_device(n, exterior_map, couple_maps, face_from_exterior, face_maps, start_inverse):
    block, width = face_from_exterior.shape
    half = face_maps.shape[0] // 2
    exterior = n * block
    group = 4 * block
    tile = tile_width(group if group % LANES == 0 else exterior)
    anywhere = pl.BlockSpec(memory_space=pl.ANY)
    in_vmem = pl.BlockSpec(memory_space=pltpu.VMEM)
    out_shape = jax.ShapeDtypeStruct((2, exterior_map.shape[0], exterior), BF16)
    return pl.pallas_call(
        functools.partial(kernel, n),
        out_shape=out_shape,
        in_specs=[anywhere, anywhere, anywhere, in_vmem, anywhere],
        out_specs=anywhere,
        scratch_shapes=[
            pltpu.VMEM((exterior, width), BF16),
            pltpu.VMEM((width, width), BF16),
            pltpu.VMEM(exterior_map.shape, BF16),
            pltpu.VMEM(couple_maps.shape, BF16),
            pltpu.VMEM((width, width), F32),
            pltpu.VMEM((width, width), BF16),
            pltpu.VMEM((width, width), BF16),
            pltpu.VMEM(couple_maps.shape, F32),
            pltpu.VMEM(couple_maps.shape, BF16),
            pltpu.VMEM((width, width), BF16),
            pltpu.VMEM((2, 2, exterior_map.shape[0], tile), BF16),
            pltpu.VMEM((half, width), BF16),
            pltpu.VMEM((half, width), BF16),
            pltpu.SemaphoreType.DMA((4,)),
            pltpu.SemaphoreType.DMA((2,)),
            pltpu.SemaphoreType.DMA((2,)),
            pltpu.SemaphoreType.DMA((2, 5, n // 4)),
            pltpu.SemaphoreType.DMA((2, n)),
        ],
        compiler_params=pltpu.CompilerParams(
            collective_id=0, has_side_effects=True, vmem_limit_bytes=60 * 1024 * 1024
        ),
    )(exterior_map, couple_maps, face_from_exterior, face_maps, start_inverse)


def solution(mesh):
    return jax.shard_map(
        functools.partial(per_device, mesh.shape["row"]),
        mesh=mesh,
        in_specs=(
            P(("groups", "row"), None),
            P("groups", "row", None),
            P(("groups", "row"), None),
            P(("groups", "row"), None),
            P("groups", None),
        ),
        out_specs=P(None, ("groups", "row"), None),
        check_vma=False,
    )
```

time: 243 us -> 135 us (0.56)
  waiting for transfers between devices: 143 us -> 0 us
  Pallas kernels: 0 us -> 120 us
  matrix products: 52.8 us -> 0 us
  other arithmetic: 23.9 us -> 0 us
  between operations: 13.5 us -> 0.01 us
  local copies, waits for them, and re-layouts: 5.75 us -> 12.6 us
  starting transfers between devices: 4.15 us -> 0 us
    all_gather x2 -> x0, waiting for transfers between devices: 136 us -> none  [the longest x1 102 us: per_device(): panels = lax.all_gather(face_from_exterior, 'row', axis=0, tiled=True)]
    pallas_call x0 -> x1, Pallas kernels: none -> 120 us  [per_device(): pl.pallas_call(functools.partial(kernel, n), out_shape=out_shape, in_spec...]
    dot_general x5 -> x0, matrix products: 52.8 us -> none  [the longest x1 22.8 us: per_device(): update = jnp.einsum('bis,es->bie', left, panels, preferred_element_type=f32)]
    another operation x3 -> x0, other arithmetic: 23.9 us -> none  [the longest x2 14.3 us: per_device(): jnp.stack([exterior_map.astype(f32) - update[0], -update[1]]).astype(bf16)]
    unnamed x10 -> x1, local copies, waits for them, and re-layouts: 2.73 us -> 12.6 us
    ppermute x1 -> x0, waiting for transfers between devices: 6.3 us -> none  [per_device(): received = lax.ppermute(theirs.astype(bf16), 'row', route).astype(f32)]
    ppermute x1 -> x0, starting transfers between devices: 4.1 us -> none  [per_device(): received = lax.ppermute(theirs.astype(bf16), 'row', route).astype(f32)]
  transfers between devices with their start and end apart: 3 -> 0, of which waited for: 3 -> 0; matrix products, arithmetic and copies ran while one was open for 11% -> 0% of each run, Pallas kernels for 0% -> 0%
where the time goes in v2:
time: 135 us; the launch traced here: 133 us
  Pallas kernels  120 us (89%)
  local copies, waits for them, and re-layouts  12.6 us (9%)
    pallas_call x1, Pallas kernels, per_device(): pl.pallas_call(functools.partial(kernel, n), out_shape=out_shape, in_spec...  120 us
    unnamed x1, local copies, waits for them, and re-layouts  12.6 us

profile of v2, /device:TPU:0, one launch (start us, length us, event | category | flops | bytes accessed | tf_op | source)
XLA Modules:
  0.0 133.1 jit_solution(7309133375852702517)
XLA Ops:
  0.0 120.4 %shard_map.55 = bf16[2,480,7680]{2,1,0:T(8,128)(2,1)} custom-call(bf16[480,7680]{1,0:T(8,128)(2,1)} %ext_ref.1, bf16[2,480,1024]{2,1,0:T(8,128)(2,1)} %maps_ref.1, bf16[480,1024]{1,0:T(8,128)(2,1)} %panel_ref.1, f32[128,1024]{1,0:T(8,128)} %face_ref.1, f32[1024,1024]{1,0:T(8,128)} %start_ref.1), custom_call_target="tpu_custom_call" | custom-call | tf_op jit(solution)/shard_map/pallas_call | solution.py:331
  120.4 12.6 %copy.7 = bf16[2,480,7680]{2,1,0:T(8,128)(2,1)} copy(bf16[2,480,7680]{2,1,0:T(8,128)(2,1)} %shard_map.55) | data formatting | bytes 29491200

commit v3 on v2

v3 whole, which is shorter than its diff:
```python
import functools

import jax
import jax.numpy as jnp
from jax import lax
from jax.experimental import pallas as pl
from jax.experimental.pallas import tpu as pltpu
from jax.sharding import PartitionSpec as P

F32 = jnp.float32
BF16 = jnp.bfloat16
LANES = 128
CHUNKS = 3
RIGHT, LEFT, RIGHT_OTHER, LEFT_OTHER, ACROSS, CORE_OWN, CORE_OTHER = range(7)


def halves(span):
    first = -(-span // (2 * LANES)) * LANES
    return ((0, first), (first, span - first)) if span > first else ((0, span),)


def kernel(
    n,
    ext_ref,
    maps_ref,
    panel_ref,
    face_ref,
    start_ref,
    out_ref,
    panels,
    resid,
    ext,
    maps,
    start,
    start_hi,
    start_lo,
    image,
    left,
    square,
    stage,
    face_out,
    face_in,
    local_sem,
    out_sem,
    face_sem,
    send_sem,
    recv_sem,
):
    line = n // 4
    halfway = n // 2
    block = panel_ref.shape[0]
    half = face_ref.shape[0] // 2
    width = start.shape[0]
    me = lax.axis_index("row")
    z, y, c = me // 4, (me // 2) % 2, me % 2
    side = me // halfway
    sibling = (me + halfway) % n
    has_right, has_left = z < line - 1, z > 0

    def device(zz, yy, cc):
        return zz * 4 + yy * 2 + cc

    local = [
        pltpu.make_async_copy(start_ref, start, local_sem.at[0]),
        pltpu.make_async_copy(maps_ref, maps, local_sem.at[1]),
        pltpu.make_async_copy(
            panel_ref,
            panels.at[pl.ds(pl.multiple_of(me * block, 16), block)],
            local_sem.at[2],
        ),
        pltpu.make_async_copy(ext_ref, ext, local_sem.at[3]),
    ]
    for copy in local:
        copy.start()

    barrier = pltpu.get_barrier_semaphore()

    def greet(target):
        pl.semaphore_signal(
            barrier, inc=1, device_id={"row": target}, device_id_type=pl.DeviceIdType.MESH
        )

    greet(device(z, 1 - y, c))
    greet(device(z, y, 1 - c))
    greet(sibling)

    @pl.when(has_right)
    def _():
        greet(me + 4)

    @pl.when(has_left)
    def _():
        greet(me - 4)

    face_out[...] = face_ref[pl.ds(pl.multiple_of((1 - side) * half, 16), half)].astype(BF16)
    pl.semaphore_wait(barrier, 3 + has_right.astype(jnp.int32) + has_left.astype(jnp.int32))

    exchange = pltpu.make_async_remote_copy(
        src_ref=face_out,
        dst_ref=face_in,
        send_sem=face_sem.at[0],
        recv_sem=face_sem.at[1],
        device_id={"row": sibling},
        device_id_type=pl.DeviceIdType.MESH,
    )
    exchange.start()

    chunk = block // CHUNKS

    def panel_rows(dev, part):
        return panels.at[pl.ds(pl.multiple_of(dev * block + part * chunk, 16), chunk)]

    def resid_start(dev):
        return pl.multiple_of((2 * (dev % halfway) + dev // halfway) * half, 16)

    def resid_rows(dev, part):
        return resid.at[pl.ds(resid_start(dev), half)]

    rows_of = (panel_rows, resid_rows)

    def copy_of(kind, way, dev, part, source=None):
        target = {
            RIGHT: me + 4,
            LEFT: me - 4,
            RIGHT_OTHER: me + 4,
            LEFT_OTHER: me - 4,
            ACROSS: device(z, 1 - y, c),
            CORE_OWN: device(z, y, 1 - c),
            CORE_OTHER: device(z, y, 1 - c),
        }[way]
        rows = rows_of[kind](dev, part)
        return pltpu.make_async_remote_copy(
            src_ref=rows if source is None else source,
            dst_ref=rows,
            send_sem=send_sem.at[kind, way, dev // 4, part],
            recv_sem=recv_sem.at[kind, dev, part],
            device_id={"row": target},
            device_id_type=pl.DeviceIdType.MESH,
        )

    def await_block(kind, dev, part):
        copy_of(kind, CORE_OWN, dev, part).wait_recv()

    def at_step(step, act):
        if step == 0:
            act(z)
        else:

            @pl.when(z >= step)
            def _():
                act(z - step)

            @pl.when(z + step < line)
            def _():
                act(z + step)

    def send_right(kind, way, dev, part, source=None):
        @pl.when(has_right)
        def _():
            copy_of(kind, way, dev, part, source).start()

    def send_left(kind, way, dev, part, source=None):
        @pl.when(has_left)
        def _():
            copy_of(kind, way, dev, part, source).start()

    def along(step, act):
        @pl.when(z >= step)
        def _():
            act(z - step, send_right, (RIGHT, RIGHT_OTHER))

        @pl.when(z + step < line)
        def _():
            act(z + step, send_left, (LEFT, LEFT_OTHER))

    def panel_send():
        for part in range(CHUNKS):
            source = panel_ref.at[pl.ds(part * chunk, chunk)]
            copy_of(0, ACROSS, me, part, source).start()
            send_right(0, RIGHT, me, part, source)
            send_left(0, LEFT, me, part, source)
            copy_of(0, CORE_OWN, me, part, source).start()

    def panel_along(step, part):
        def act(zz, send, ways):
            dev = device(zz, y, c)
            await_block(0, dev, part)
            send(0, ways[0], dev, part)
            copy_of(0, ACROSS, dev, part).start()
            copy_of(0, CORE_OWN, dev, part).start()

        along(step, act)

    def panel_across(step):
        def act(zz):
            for part in range(CHUNKS):
                dev = device(zz, 1 - y, c)
                await_block(0, dev, part)
                copy_of(0, CORE_OTHER, dev, part).start()

        at_step(step, act)

    def panel_core(step, column):
        def act(zz):
            for part in range(CHUNKS):
                await_block(0, device(zz, column, 1 - c), part)

        at_step(step, act)

    def resid_across():
        dev = device(z, 1 - y, c)
        await_block(1, dev, 0)
        send_right(1, RIGHT_OTHER, dev, 0)
        send_left(1, LEFT_OTHER, dev, 0)
        copy_of(1, CORE_OTHER, dev, 0).start()

    def resid_along(step):
        def act(zz, send, ways):
            dev = device(zz, y, c)
            await_block(1, dev, 0)
            send(1, ways[0], dev, 0)
            copy_of(1, CORE_OWN, dev, 0).start()
            dev = device(zz, 1 - y, c)
            await_block(1, dev, 0)
            send(1, ways[1], dev, 0)
            copy_of(1, CORE_OTHER, dev, 0).start()

        along(step, act)

    def resid_core(step):
        def act(zz):
            await_block(1, device(zz, y, 1 - c), 0)
            await_block(1, device(zz, 1 - y, 1 - c), 0)

        at_step(step, act)

    def finish():
        @pl.loop(0, line)
        def _(zz):
            own, other = device(zz, y, c), device(zz, 1 - y, c)

            @pl.when(has_right & (zz <= z))
            def _():
                for part in range(CHUNKS):
                    copy_of(0, RIGHT, own, part).wait_send()
                copy_of(1, RIGHT, own, 0).wait_send()
                copy_of(1, RIGHT_OTHER, other, 0).wait_send()

            @pl.when(has_left & (zz >= z))
            def _():
                for part in range(CHUNKS):
                    copy_of(0, LEFT, own, part).wait_send()
                copy_of(1, LEFT, own, 0).wait_send()
                copy_of(1, LEFT_OTHER, other, 0).wait_send()

            for part in range(CHUNKS):
                copy_of(0, ACROSS, own, part).wait_send()
                copy_of(0, CORE_OWN, own, part).wait_send()
                copy_of(0, CORE_OTHER, other, part).wait_send()
            copy_of(1, CORE_OWN, own, 0).wait_send()
            copy_of(1, CORE_OTHER, other, 0).wait_send()

        copy_of(1, ACROSS, me, 0).wait_send()

    panel_send()

    local[0].wait()
    local[1].wait()
    start_hi[...] = start[...].astype(BF16)
    start_lo[...] = (start[...] - start_hi[...].astype(F32)).astype(BF16)

    @pl.loop(0, 2)
    def _(box):
        image[box] = jnp.dot(
            maps[box], start_hi[...], preferred_element_type=F32
        ) + jnp.dot(maps[box], start_lo[...], preferred_element_type=F32)

    exchange.wait()
    coupling = face_ref[pl.ds(pl.multiple_of(side * half, 16), half)] + face_in[...].astype(F32)
    coupling_hi = coupling.astype(BF16)
    coupling_lo = (coupling - coupling_hi.astype(F32)).astype(BF16)
    product = jnp.dot(coupling_hi, start_hi[...], preferred_element_type=F32)
    product += jnp.dot(coupling_hi, start_lo[...], preferred_element_type=F32)
    product += jnp.dot(coupling_lo, start_hi[...], preferred_element_type=F32)
    first = resid_start(me)
    row_index = first + lax.broadcasted_iota(jnp.int32, product.shape, 0)
    col_index = lax.broadcasted_iota(jnp.int32, product.shape, 1)
    identity = jnp.where(row_index == col_index, 1.0, 0.0)
    resid[pl.ds(first, half)] = (identity - product).astype(BF16)
    copy_of(1, ACROSS, me, 0).start()
    send_right(1, RIGHT, me, 0)
    send_left(1, LEFT, me, 0)
    copy_of(1, CORE_OWN, me, 0).start()

    panel_along(1, 0)
    panel_along(1, 1)
    resid_across()
    panel_along(1, 2)
    for step in range(1, line):
        resid_along(step)
    for step in range(line):
        resid_core(step)
    if line > 2:
        panel_along(2, 0)

    square_rows = width // 4

    @pl.loop(0, 4)
    def _(part):
        rows = pl.ds(pl.multiple_of(part * square_rows, 16), square_rows)
        square[rows] = jnp.dot(resid[rows], resid[...], preferred_element_type=F32).astype(BF16)

    @pl.loop(0, 2)
    def _(box):
        value = image[box]
        value += jnp.dot(value.astype(BF16), resid[...], preferred_element_type=F32)
        value += jnp.dot(value.astype(BF16), square[...], preferred_element_type=F32)
        left[box] = value.astype(BF16)

    if line > 2:
        panel_along(2, 1)
    local[2].wait()
    local[3].wait()

    def columns(begin, spans):
        copies = []
        for slot, (offset, tile) in enumerate(spans):
            at = pl.multiple_of(begin + offset, LANES)
            part = panels[pl.ds(at, tile)]
            contract = (((1,), (1,)), ((), ()))
            upper = lax.dot_general(left[0], part, contract, preferred_element_type=F32)
            mine = (ext[:, pl.ds(at, tile)].astype(F32) - upper).astype(BF16)
            stage[slot, 0, :, pl.ds(0, tile)] = mine
            lower = lax.dot_general(left[1], part, contract, preferred_element_type=F32)
            stage[slot, 1, :, pl.ds(0, tile)] = (-lower).astype(BF16)
            copies.append(
                pltpu.make_async_copy(
                    stage.at[slot, :, :, pl.ds(0, tile)],
                    out_ref.at[:, :, pl.ds(at, tile)],
                    out_sem.at[slot],
                )
            )
            copies[-1].start()
        for copy in copies:
            copy.wait()

    group = 4 * block
    aligned = group % LANES == 0
    early_width = 2 * block // LANES * LANES
    late_width = group - early_width

    def early(step):
        panel_core(step, y)
        if aligned:
            begin = y * late_width
            at_step(step, lambda zz: columns(zz * group + begin, halves(early_width)))

    def late(step):
        panel_core(step, 1 - y)
        if aligned:
            begin = (1 - y) * early_width
            at_step(step, lambda zz: columns(zz * group + begin, halves(late_width)))

    early(0)
    if line > 2:
        panel_along(2, 2)
    panel_across(0)
    late(0)
    for step in range(1, line):
        early(step)
        if step > 2 and step + 1 < line:
            panel_along(step + 1, 0)
            panel_along(step + 1, 1)
            panel_along(step + 1, 2)
        panel_across(step)
        late(step)
        if step == 1 and line > 3:
            for part in range(CHUNKS):
                panel_along(3, part)
    if not aligned:
        span = 2 * LANES

        @pl.loop(0, panels.shape[0] // span)
        def _(index):
            columns(index * span, ((0, span),))

    finish()


def per_device(n, exterior_map, couple_maps, face_from_exterior, face_maps, start_inverse):
    block, width = face_from_exterior.shape
    half = face_maps.shape[0] // 2
    exterior = n * block
    tile = max(2 * LANES, -(-2 * block // LANES // 2) * LANES)
    anywhere = pl.BlockSpec(memory_space=pl.ANY)
    in_vmem = pl.BlockSpec(memory_space=pltpu.VMEM)
    out_shape = jax.ShapeDtypeStruct((2, exterior_map.shape[0], exterior), BF16)
    return pl.pallas_call(
        functools.partial(kernel, n),
        out_shape=out_shape,
        in_specs=[anywhere, anywhere, anywhere, in_vmem, anywhere],
        out_specs=anywhere,
        scratch_shapes=[
            pltpu.VMEM((exterior, width), BF16),
            pltpu.VMEM((width, width), BF16),
            pltpu.VMEM(exterior_map.shape, BF16),
            pltpu.VMEM(couple_maps.shape, BF16),
            pltpu.VMEM((width, width), F32),
            pltpu.VMEM((width, width), BF16),
            pltpu.VMEM((width, width), BF16),
            pltpu.VMEM(couple_maps.shape, F32),
            pltpu.VMEM(couple_maps.shape, BF16),
            pltpu.VMEM((width, width), BF16),
            pltpu.VMEM((2, 2, exterior_map.shape[0], tile), BF16),
            pltpu.VMEM((half, width), BF16),
            pltpu.VMEM((half, width), BF16),
            pltpu.SemaphoreType.DMA((4,)),
            pltpu.SemaphoreType.DMA((2,)),
            pltpu.SemaphoreType.DMA((2,)),
            pltpu.SemaphoreType.DMA((2, 7, n // 4, CHUNKS)),
            pltpu.SemaphoreType.DMA((2, n, CHUNKS)),
        ],
        compiler_params=pltpu.CompilerParams(
            collective_id=0, has_side_effects=True, vmem_limit_bytes=60 * 1024 * 1024
        ),
    )(exterior_map, couple_maps, face_from_exterior, face_maps, start_inverse)


def solution(mesh):
    return jax.shard_map(
        functools.partial(per_device, mesh.shape["row"]),
        mesh=mesh,
        in_specs=(
            P(("groups", "row"), None),
            P("groups", "row", None),
            P(("groups", "row"), None),
            P(("groups", "row"), None),
            P("groups", None),
        ),
        out_specs=P(None, ("groups", "row"), None),
        check_vma=False,
    )
```

time: 135 us -> 140 us (1.037); the launches traced: 133 us -> 140 us
  Pallas kernels: 120 us -> 127 us
    pallas_call x1, Pallas kernels: 120 us -> 127 us  [per_device(): pl.pallas_call(functools.partial(kernel, n), out_shape=out_shape, in_spec...]
where the time goes in v3:
time: 140 us
  Pallas kernels  127 us (91%)
  local copies, waits for them, and re-layouts  12.6 us (9%)
    pallas_call x1, Pallas kernels, per_device(): pl.pallas_call(functools.partial(kernel, n), out_shape=out_shape, in_spec...  127 us
    unnamed x1, local copies, waits for them, and re-layouts  12.6 us

profile of v3, /device:TPU:0, one launch (start us, length us, event | category | flops | bytes accessed | tf_op | source)
XLA Modules:
  0.0 140.1 jit_solution(2266804031698763458)
XLA Ops:
  0.0 127.4 %shard_map.55 = bf16[2,480,7680]{2,1,0:T(8,128)(2,1)} custom-call(bf16[480,7680]{1,0:T(8,128)(2,1)} %ext_ref.1, bf16[2,480,1024]{2,1,0:T(8,128)(2,1)} %maps_ref.1, bf16[480,1024]{1,0:T(8,128)(2,1)} %panel_ref.1, f32[128,1024]{1,0:T(8,128)} %face_ref.1, f32[1024,1024]{1,0:T(8,128)} %start_ref.1), custom_call_target="tpu_custom_call" | custom-call | tf_op jit(solution)/shard_map/pallas_call | solution.py:398
  127.4 12.6 %copy.7 = bf16[2,480,7680]{2,1,0:T(8,128)(2,1)} copy(bf16[2,480,7680]{2,1,0:T(8,128)(2,1)} %shard_map.55) | data formatting | bytes 29491200

commit v4 on v2

--- a/solution.py
+++ b/solution.py
@@ -103,8 +103,14 @@
     )
     exchange.start()
 
-    def panel_rows(dev):
-        return panels.at[pl.ds(pl.multiple_of(dev * block, 16), block)]
+    front = block // 32 * 16
+    back = block - front
+
+    def front_rows(dev):
+        return panels.at[pl.ds(pl.multiple_of(dev * block, 16), front)]
+
+    def back_rows(dev):
+        return panels.at[pl.ds(pl.multiple_of(dev * block + front, 16), back)]
 
     def resid_start(dev):
         return pl.multiple_of((2 * (dev % halfway) + dev // halfway) * half, 16)
@@ -218,10 +224,11 @@
 
         return send_own, along, across, core, finish, at_step
 
-    send_panel, panel_along, panel_across, panel_core, panel_finish, at_step = relay(0, panel_rows)
+    send_front, front_along, front_across, front_core, front_finish, at_step = relay(0, front_rows)
+    send_back, back_along, back_across, back_core, back_finish, _ = relay(2, back_rows)
     send_resid, resid_along, resid_across, resid_core, resid_finish, _ = relay(1, resid_rows)
 
-    send_panel(panel_ref)
+    send_front(panel_ref.at[pl.ds(0, front)])
 
     local[0].wait()
     start_hi[...] = start[...].astype(BF16)
@@ -240,6 +247,11 @@
     resid[pl.ds(first, half)] = (identity - product).astype(BF16)
     send_resid(resid_rows(me))
 
+    for step in range(1, line):
+        resid_along(step)
+    send_back(panel_ref.at[pl.ds(front, back)])
+    front_along(1)
+
     local[1].wait()
 
     @pl.loop(0, 2)
@@ -248,13 +260,11 @@
             maps[box], start_hi[...], preferred_element_type=F32
         ) + jnp.dot(maps[box], start_lo[...], preferred_element_type=F32)
 
-    for step in range(1, line):
-        resid_along(step)
-    panel_along(1)
     for step in range(line):
         resid_across(step)
     for step in range(line):
         resid_core(step)
+    back_along(1)
 
     square_rows = width // 4
 
@@ -270,6 +280,8 @@
         value += jnp.dot(value.astype(BF16), square[...], preferred_element_type=F32)
         left[box] = value.astype(BF16)
 
+    if line > 2:
+        front_along(2)
     local[2].wait()
     local[3].wait()
 
@@ -307,15 +319,20 @@
     aligned = group % LANES == 0
     for step in range(line):
         if step > 0 and step + 1 < line:
-            panel_along(step + 1)
-        panel_across(step)
-        panel_core(step)
+            if step > 1:
+                front_along(step + 1)
+            back_along(step + 1)
+        front_across(step)
+        back_across(step)
+        front_core(step)
+        back_core(step)
         if aligned:
             at_step(step, lambda zz: columns(zz * group, group))
     if not aligned:
         columns(0, panels.shape[0])
 
-    panel_finish()
+    front_finish()
+    back_finish()
     resid_finish()
 
 
@@ -350,8 +367,8 @@
             pltpu.SemaphoreType.DMA((4,)),
             pltpu.SemaphoreType.DMA((2,)),
             pltpu.SemaphoreType.DMA((2,)),
-            pltpu.SemaphoreType.DMA((2, 5, n // 4)),
-            pltpu.SemaphoreType.DMA((2, n)),
+            pltpu.SemaphoreType.DMA((3, 5, n // 4)),
+            pltpu.SemaphoreType.DMA((3, n)),
         ],
         compiler_params=pltpu.CompilerParams(
             collective_id=0, has_side_effects=True, vmem_limit_bytes=60 * 1024 * 1024

time: 135 us -> 134 us (level)
  no operation moved by 1% of the time
where the time goes in v4:
time: 134 us; the launch traced here: 133 us
  Pallas kernels  120 us (90%)
  local copies, waits for them, and re-layouts  12.6 us (9%)
    pallas_call x1, Pallas kernels, per_device(): pl.pallas_call(functools.partial(kernel, n), out_shape=out_shape, in_spec...  120 us
    unnamed x1, local copies, waits for them, and re-layouts  12.6 us

profile of v4, /device:TPU:0, one launch (start us, length us, event | category | flops | bytes accessed | tf_op | source)
XLA Modules:
  0.0 132.7 jit_solution(13610154871897395469)
XLA Ops:
  0.0 120.1 %shard_map.55 = bf16[2,480,7680]{2,1,0:T(8,128)(2,1)} custom-call(bf16[480,7680]{1,0:T(8,128)(2,1)} %ext_ref.1, bf16[2,480,1024]{2,1,0:T(8,128)(2,1)} %maps_ref.1, bf16[480,1024]{1,0:T(8,128)(2,1)} %panel_ref.1, f32[128,1024]{1,0:T(8,128)} %face_ref.1, f32[1024,1024]{1,0:T(8,128)} %start_ref.1), custom_call_target="tpu_custom_call" | custom-call | tf_op jit(solution)/shard_map/pallas_call | solution.py:348
  120.1 12.6 %copy.7 = bf16[2,480,7680]{2,1,0:T(8,128)(2,1)} copy(bf16[2,480,7680]{2,1,0:T(8,128)(2,1)} %shard_map.55) | data formatting | bytes 29491200
